TPU v7x, 32 devices: a whole 2x2x4 slice. The times are simulated.
32 devices in a mesh: dp: 2 (over core), cuts: 4 (over y, x), topic: 4 (over z).
Axes of the slice: x: 2, y: 2, z: 4, core: 2. Of those that a mesh axis runs over, the one named last changes fastest.
Arguments:
- doc_mix: float32 [2048, 4096], P(('dp', 'cuts'), 'topic'), may hold values from 0.01 to 1
- doc_lengths: int32 [2048], P(('dp', 'cuts')), may hold values from 1 to 4096, 524288 in all
- counts: int32 [2048, 256], P(('dp', 'cuts')), may hold values from 0 to 7
- tile_on: int32 [8, 4], P(('dp', 'cuts')), may hold values from 0 to 1, as said below
- word_counts: float32 [256, 4096], P('cuts', 'topic'), may hold values from 0.01 to 10
- topic_totals: float32 [4096], P('topic'), may hold values from 1000 to 100000
Outputs:
- doc_topic: float32 [2048, 4096], P(('dp', 'cuts'), 'topic')
- word_topic: float32 [256, 4096], P('cuts', 'topic')
Inputs may be any that keep to these rules, and one draw needn't show every extreme that they name: `tile_on`: each block of documents meets at least one word slice.
All inputs are finite; a program needn't handle non-finite values. No bound on the sum of `doc_lengths` on one device may be relied on, other than what follows from the above.
Results may differ from a plain program's by a relative error of at most 0.000078.
Values sent between devices are 32-bit elements; how exact they have to be, the bound alone decides.
A program may use at most 64 MiB of HBM per device.

v0:
```python
import jax
import jax.numpy as jnp
from jax import lax
from jax.sharding import PartitionSpec as P

VOCAB = 1048576


ALPHA = 0.1
BETA = 0.01


def passed_along(block, axis, distance):
    devices = range(lax.axis_size(axis))
    route = [((i - distance) % len(devices), i) for i in devices]
    return lax.ppermute(block, axis, route)


def matmul_high(left, right):
    return jnp.dot(left, right, precision=lax.Precision.HIGHEST, preferred_element_type=jnp.float32)


def slice_ratio(doc_weight, word_weight, weights):
    partial_denom = matmul_high(doc_weight, word_weight.T)
    share_rows = doc_weight.shape[0] // lax.axis_size("topic")
    denom_share = lax.psum_scatter(partial_denom, "topic", scatter_dimension=0, tiled=True)
    weight_share = lax.dynamic_slice_in_dim(
        weights, lax.axis_index("topic") * share_rows, share_rows, 0
    )
    return lax.all_gather(weight_share / denom_share, "topic", axis=0, tiled=True)


def shards(doc_mix, doc_lengths, counts, tile_on, word_counts, topic_totals):
    mass = lax.psum(jnp.sum(doc_mix, axis=1), "topic")
    doc_weight = doc_lengths.astype(jnp.float32)[:, None] * doc_mix / mass[:, None] + ALPHA
    word_home = (word_counts + BETA) / (topic_totals + VOCAB * BETA)[None, :]
    slice_words = word_home.shape[0]
    slice_count = lax.axis_size("cuts")
    own_index = lax.axis_index("cuts")
    tile_row = tile_on[0]

    def slice_weights(slice_index):
        block = lax.dynamic_slice_in_dim(counts, slice_index * slice_words, slice_words, 1)
        flag = lax.dynamic_index_in_dim(tile_row, slice_index, 0, keepdims=False)
        return (block * flag).astype(jnp.float32)

    doc_sums = jnp.zeros(doc_weight.shape, jnp.float32)

    def one_round(round_index, carry):
        doc_acc, word_weight, word_acc = carry
        slice_index = (own_index - round_index) % slice_count
        ratio = slice_ratio(doc_weight, word_weight, slice_weights(slice_index))
        doc_acc = doc_acc + matmul_high(ratio, word_weight)
        word_acc = word_acc + matmul_high(ratio.T, doc_weight)
        word_weight, word_acc = passed_along((word_weight, word_acc), "cuts", 1)
        return (doc_acc, word_weight, word_acc)

    start = (doc_sums, word_home, jnp.zeros(word_home.shape, jnp.float32))
    doc_sums, moved_home, word_local = lax.fori_loop(0, slice_count, one_round, start)
    word_total = lax.psum(word_local, "dp")
    return (doc_weight * doc_sums, word_home * word_total)


def solution(mesh):
    return jax.shard_map(
        shards,
        mesh=mesh,
        in_specs=(
            P(("dp", "cuts"), "topic"),
            P(("dp", "cuts")),
            P(("dp", "cuts"), None),
            P(("dp", "cuts"), None),
            P("cuts", "topic"),
            P("topic"),
        ),
        out_specs=(P(("dp", "cuts"), "topic"), P("cuts", "topic")),
        check_vma=False,
    )
```

profile of v0, /device:TPU:0, one launch (start us, length us, event | category | flops | bytes accessed | tf_op | source)
XLA Modules:
  0.0 232.0 jit_solution(12932590767569357858)
XLA Ops:
  8.0 0.7 copy-done.3
  8.7 1.4 reduce_sum.9
  10.1 13.5 %psum.14 = f32[256]{0:T(256)S(1)} all-reduce(f32[256]{0:T(256)S(1)} %reduce_sum.9), channel_id=1, replica_groups=mesh['dp'=2,'cuts'=4,'topic'=4] {'topic'}, use_global_device_ids=true, to_apply=%region_1.0 | all-reduce | flops 256 | bytes 2048 | tf_op jit(solution)/shard_map/psum | solution.py:34
  23.6 1.4 divide_add_fusion
  25.1 0.6 copy-done.4
  25.7 178.9 %while.20 = (s32[]{:T(128)}, f32[256,1024]{1,0:T(8,128)S(1)}, f32[64,1024]{1,0:T(8,128)S(1)}, f32[64,1024]{1,0:T(8,128)S(1)}, s32[]{:T(128)}, /*index=5*/s32[256...) while((s32[]{:T(128)}, f32[256,1024]{1,0:T(8,128)S(1)}, ...), condition=%wide.region_4.5_spmd.clone, body=%wide.region_2.4_spmd.clone.sunk | while | flops 604581888 | bytes 8520242 | solution.py:59
  25.7 1.6 fusion.25
  27.4 1.5 collective-permute-start
  28.9 0.6 dynamic_slice.35
  29.5 17.4 %reduce-scatter.2.cloned.1.call-done = f32[64,64]{1,0:T(8,128)} async-done(((f32[256,64]{1,0:T(8,128)}), f32[64,64]{1,0:T(8,128)}) %reduce-scatter.2.cloned.1.call-update) | async-done | bytes 16400 | tf_op jit(solution)/shard_map/while/body/eval_jaxpr/reduce_scatter | solution.py:26
  46.9 1.4 fusion.26
  48.3 13.4 %all_gather.12 = f32[256,64]{1,0:T(8,128)S(1)} all-gather(f32[64,64]{1,0:T(8,128)S(1)} %fusion.26), channel_id=1, replica_groups=mesh['dp'=2,'cuts'=4,'topic'=4] {'topic'}, dimensions={0}, use_global_device_ids=true | all-gather | bytes 81920 | tf_op jit(solution)/shard_map/while/body/eval_jaxpr/all_gather | solution.py:30
  61.6 0.8 convolution_add_fusion.5
  62.4 1.5 collective-permute-start.1
  63.9 1.1 convolution_add_fusion.4
  65.1 5.4 %collective-permute-done.1 = f32[64,1024]{1,0:T(8,128)S(1)} collective-permute-done((f32[64,1024]{1,0:T(8,128)S(1)}, f32[64,1024]{1,0:T(8,128)S(1)}, u32[]{:S(2)}, u32[]{:S(2)}) %collective-permute-start.1) | collective-permute-done | bytes 262176 | tf_op jit(solution)/shard_map/while/body/eval_jaxpr/ppermute | solution.py:16
  70.6 1.6 fusion.25
  72.2 1.8 collective-permute-start
  74.5 17.2 %reduce-scatter.2.cloned.1.call-done = f32[64,64]{1,0:T(8,128)} async-done(((f32[256,64]{1,0:T(8,128)}), f32[64,64]{1,0:T(8,128)}) %reduce-scatter.2.cloned.1.call-update) | async-done | bytes 16400 | tf_op jit(solution)/shard_map/while/body/eval_jaxpr/reduce_scatter | solution.py:26
  91.7 1.4 fusion.26
  93.2 13.4 %all_gather.12 = f32[256,64]{1,0:T(8,128)S(1)} all-gather(f32[64,64]{1,0:T(8,128)S(1)} %fusion.26), channel_id=1, replica_groups=mesh['dp'=2,'cuts'=4,'topic'=4] {'topic'}, dimensions={0}, use_global_device_ids=true | all-gather | bytes 81920 | tf_op jit(solution)/shard_map/while/body/eval_jaxpr/all_gather | solution.py:30
  106.5 0.8 convolution_add_fusion.5
  107.3 1.5 collective-permute-start.1
  108.8 1.1 convolution_add_fusion.4
  110.0 5.4 %collective-permute-done.1 = f32[64,1024]{1,0:T(8,128)S(1)} collective-permute-done((f32[64,1024]{1,0:T(8,128)S(1)}, f32[64,1024]{1,0:T(8,128)S(1)}, u32[]{:S(2)}, u32[]{:S(2)}) %collective-permute-start.1) | collective-permute-done | bytes 262176 | tf_op jit(solution)/shard_map/while/body/eval_jaxpr/ppermute | solution.py:16
  115.4 1.6 fusion.25
  117.1 1.7 collective-permute-start
  119.3 17.3 %reduce-scatter.2.cloned.1.call-done = f32[64,64]{1,0:T(8,128)} async-done(((f32[256,64]{1,0:T(8,128)}), f32[64,64]{1,0:T(8,128)}) %reduce-scatter.2.cloned.1.call-update) | async-done | bytes 16400 | tf_op jit(solution)/shard_map/while/body/eval_jaxpr/reduce_scatter | solution.py:26
  136.6 1.4 fusion.26
  138.0 13.4 %all_gather.12 = f32[256,64]{1,0:T(8,128)S(1)} all-gather(f32[64,64]{1,0:T(8,128)S(1)} %fusion.26), channel_id=1, replica_groups=mesh['dp'=2,'cuts'=4,'topic'=4] {'topic'}, dimensions={0}, use_global_device_ids=true | all-gather | bytes 81920 | tf_op jit(solution)/shard_map/while/body/eval_jaxpr/all_gather | solution.py:30
  151.4 0.8 convolution_add_fusion.5
  152.2 1.4 collective-permute-start.1
  153.6 1.1 convolution_add_fusion.4
  154.7 5.5 %collective-permute-done.1 = f32[64,1024]{1,0:T(8,128)S(1)} collective-permute-done((f32[64,1024]{1,0:T(8,128)S(1)}, f32[64,1024]{1,0:T(8,128)S(1)}, u32[]{:S(2)}, u32[]{:S(2)}) %collective-permute-start.1) | collective-permute-done | bytes 262176 | tf_op jit(solution)/shard_map/while/body/eval_jaxpr/ppermute | solution.py:16
  160.3 1.6 fusion.25
  161.9 1.7 collective-permute-start
  163.6 0.6 dynamic_slice.35
  164.2 17.5 %reduce-scatter.2.cloned.1.call-done = f32[64,64]{1,0:T(8,128)} async-done(((f32[256,64]{1,0:T(8,128)}), f32[64,64]{1,0:T(8,128)}) %reduce-scatter.2.cloned.1.call-update) | async-done | bytes 16400 | tf_op jit(solution)/shard_map/while/body/eval_jaxpr/reduce_scatter | solution.py:26
  181.7 1.4 fusion.26
  183.1 13.4 %all_gather.12 = f32[256,64]{1,0:T(8,128)S(1)} all-gather(f32[64,64]{1,0:T(8,128)S(1)} %fusion.26), channel_id=1, replica_groups=mesh['dp'=2,'cuts'=4,'topic'=4] {'topic'}, dimensions={0}, use_global_device_ids=true | all-gather | bytes 81920 | tf_op jit(solution)/shard_map/while/body/eval_jaxpr/all_gather | solution.py:30
  196.5 0.8 convolution_add_fusion.5
  197.3 1.5 collective-permute-start.1
  198.8 1.1 convolution_add_fusion.4
  199.9 4.7 %collective-permute-done.1 = f32[64,1024]{1,0:T(8,128)S(1)} collective-permute-done((f32[64,1024]{1,0:T(8,128)S(1)}, f32[64,1024]{1,0:T(8,128)S(1)}, u32[]{:S(2)}, u32[]{:S(2)}) %collective-permute-start.1) | collective-permute-done | bytes 262176 | tf_op jit(solution)/shard_map/while/body/eval_jaxpr/ppermute | solution.py:16
  204.6 0.7 copy-done
  205.3 2.4 %fusion.10 = f32[256,1024]{1,0:T(8,128)} fusion(f32[256,1024]{1,0:T(8,128)S(1)} %get-tuple-element.202, f32[256]{0:T(256)S(1)} %psum.14, f32[256,1024]{1,0:T(8,128)} %param.8, f32[256]{0:T(256)S(1)} %convert_element_type.13), kind=kLoop, calls=%fused_computation.10 | loop fusion | flops 1048576 | bytes 3147776 | tf_op jit(solution)/shard_map/mul | solution.py:61
  207.7 15.5 %all-reduce.2.cloned.1.call-done = f32[64,1024]{1,0:T(8,128)} async-done(((f32[64,1024]{1,0:T(8,128)}), f32[64,1024]{1,0:T(8,128)}) %all-reduce.2.cloned.1.call-update) | async-done | bytes 262160 | tf_op jit(solution)/shard_map/psum | solution.py:60
  223.2 1.7 fusion.9
  (32 shorter events, 1.4 us)
Async XLA Ops:
  8.0 0.7 copy-start.3
  8.7 14.9 %copy-start.2 = (f32[1024]{0:T(1024)S(1)}, f32[1024]{0:T(1024)}, u32[]{:S(2)}) copy-start(f32[1024]{0:T(1024)} %param.13) | copy-start | bytes 12292
  8.7 14.9 %copy-start.1 = (f32[64,1024]{1,0:T(8,128)S(1)}, f32[64,1024]{1,0:T(8,128)}, u32[]{:S(2)}) copy-start(f32[64,1024]{1,0:T(8,128)} %param.12) | copy-start | bytes 786436
  25.0 0.7 copy-start.4
  25.7 21.2 %reduce-scatter.2.cloned.1.call-start = ((), (), s32[]{:S(2)}) async-start(), calls=%async_computation.2 | async-start | bytes 163840 | tf_op jit(solution)/shard_map/while/body/eval_jaxpr/reduce_scatter | solution.py:26
  27.4 37.7 %collective-permute-start = (f32[64,1024]{1,0:T(8,128)S(1)}, f32[64,1024]{1,0:T(8,128)S(1)}, u32[]{:S(2)}, u32[]{:S(2)}) collective-permute-start(f32[64,1024]{1,0:T(8,128)S(1)} %copy.14), channel_id=1, source_target_pairs={{12,0},{0,4},{4,8},{8,12},{13,1},{1,5},{5,9},{9,13},{14,2},{2,6},{... | collective-permute-start | bytes 786440 | tf_op jit(solution)/shard_map/while/body/eval_jaxpr/ppermute | solution.py:16
  62.4 8.1 %collective-permute-start.1 = (f32[64,1024]{1,0:T(8,128)S(1)}, f32[64,1024]{1,0:T(8,128)S(1)}, u32[]{:S(2)}, u32[]{:S(2)}) collective-permute-start(f32[64,1024]{1,0:T(8,128)S(1)} %convolution_add_fusion.5), channel_id=1, source_target_pairs={{12,0},{0,4},{4,8},{8,12},{13,1},{1,5},{5,9},{9,13},{14,2},{2,6},{... | collective-permute-start | bytes 786440 | tf_op jit(solution)/shard_map/while/body/eval_jaxpr/ppermute | solution.py:16
  70.5 21.2 %reduce-scatter.2.cloned.1.call-start = ((), (), s32[]{:S(2)}) async-start(), calls=%async_computation.2 | async-start | bytes 163840 | tf_op jit(solution)/shard_map/while/body/eval_jaxpr/reduce_scatter | solution.py:26
  72.2 37.7 %collective-permute-start = (f32[64,1024]{1,0:T(8,128)S(1)}, f32[64,1024]{1,0:T(8,128)S(1)}, u32[]{:S(2)}, u32[]{:S(2)}) collective-permute-start(f32[64,1024]{1,0:T(8,128)S(1)} %copy.14), channel_id=1, source_target_pairs={{12,0},{0,4},{4,8},{8,12},{13,1},{1,5},{5,9},{9,13},{14,2},{2,6},{... | collective-permute-start | bytes 786440 | tf_op jit(solution)/shard_map/while/body/eval_jaxpr/ppermute | solution.py:16
  107.3 8.1 %collective-permute-start.1 = (f32[64,1024]{1,0:T(8,128)S(1)}, f32[64,1024]{1,0:T(8,128)S(1)}, u32[]{:S(2)}, u32[]{:S(2)}) collective-permute-start(f32[64,1024]{1,0:T(8,128)S(1)} %convolution_add_fusion.5), channel_id=1, source_target_pairs={{12,0},{0,4},{4,8},{8,12},{13,1},{1,5},{5,9},{9,13},{14,2},{2,6},{... | collective-permute-start | bytes 786440 | tf_op jit(solution)/shard_map/while/body/eval_jaxpr/ppermute | solution.py:16
  115.4 21.2 %reduce-scatter.2.cloned.1.call-start = ((), (), s32[]{:S(2)}) async-start(), calls=%async_computation.2 | async-start | bytes 163840 | tf_op jit(solution)/shard_map/while/body/eval_jaxpr/reduce_scatter | solution.py:26
  117.1 37.7 %collective-permute-start = (f32[64,1024]{1,0:T(8,128)S(1)}, f32[64,1024]{1,0:T(8,128)S(1)}, u32[]{:S(2)}, u32[]{:S(2)}) collective-permute-start(f32[64,1024]{1,0:T(8,128)S(1)} %copy.14), channel_id=1, source_target_pairs={{12,0},{0,4},{4,8},{8,12},{13,1},{1,5},{5,9},{9,13},{14,2},{2,6},{... | collective-permute-start | bytes 786440 | tf_op jit(solution)/shard_map/while/body/eval_jaxpr/ppermute | solution.py:16
  152.2 8.1 %collective-permute-start.1 = (f32[64,1024]{1,0:T(8,128)S(1)}, f32[64,1024]{1,0:T(8,128)S(1)}, u32[]{:S(2)}, u32[]{:S(2)}) collective-permute-start(f32[64,1024]{1,0:T(8,128)S(1)} %convolution_add_fusion.5), channel_id=1, source_target_pairs={{12,0},{0,4},{4,8},{8,12},{13,1},{1,5},{5,9},{9,13},{14,2},{2,6},{... | collective-permute-start | bytes 786440 | tf_op jit(solution)/shard_map/while/body/eval_jaxpr/ppermute | solution.py:16
  160.3 21.4 %reduce-scatter.2.cloned.1.call-start = ((), (), s32[]{:S(2)}) async-start(), calls=%async_computation.2 | async-start | bytes 163840 | tf_op jit(solution)/shard_map/while/body/eval_jaxpr/reduce_scatter | solution.py:26
  161.9 38.0 %collective-permute-start = (f32[64,1024]{1,0:T(8,128)S(1)}, f32[64,1024]{1,0:T(8,128)S(1)}, u32[]{:S(2)}, u32[]{:S(2)}) collective-permute-start(f32[64,1024]{1,0:T(8,128)S(1)} %copy.14), channel_id=1, source_target_pairs={{12,0},{0,4},{4,8},{8,12},{13,1},{1,5},{5,9},{9,13},{14,2},{2,6},{... | collective-permute-start | bytes 786440 | tf_op jit(solution)/shard_map/while/body/eval_jaxpr/ppermute | solution.py:16
  197.3 7.3 %collective-permute-start.1 = (f32[64,1024]{1,0:T(8,128)S(1)}, f32[64,1024]{1,0:T(8,128)S(1)}, u32[]{:S(2)}, u32[]{:S(2)}) collective-permute-start(f32[64,1024]{1,0:T(8,128)S(1)} %convolution_add_fusion.5), channel_id=1, source_target_pairs={{12,0},{0,4},{4,8},{8,12},{13,1},{1,5},{5,9},{9,13},{14,2},{2,6},{... | collective-permute-start | bytes 786440 | tf_op jit(solution)/shard_map/while/body/eval_jaxpr/ppermute | solution.py:16
  204.6 0.7 copy-start
  204.6 18.6 %all-reduce.2.cloned.1.call-start = ((), (), s32[]{:S(2)}) async-start(), calls=%async_computation.1 | async-start | bytes 524288 | tf_op jit(solution)/shard_map/psum | solution.py:60
Sparse Core Ops, SparseCore 0:
  29.4 17.3 reduce-scatter.1
  74.3 17.4 reduce-scatter.1
  119.1 17.3 reduce-scatter.1
  163.7 17.9 reduce-scatter.1
Sparse Core Ops, SparseCore 1:
  208.0 15.2 all-reduce.1
where the time goes:
time: 233 us; the launch traced here: 232 us
  waiting for transfers between devices  106 us (45%)
  blocking collectives  67 us (29%)
  between operations  15.2 us (7%)
  matrix products  14.2 us (6%)
  other arithmetic  12.6 us (5%)
  starting transfers between devices  12.5 us (5%)
  local copies, waits for them, and re-layouts  4.4 us (2%)
    reduce_scatter x4, waiting for transfers between devices, slice_ratio(): lax.psum_scatter(partial_denom, 'topic', scatter_dimension=0, tiled=True)  69.3 us
    all_gather x4, blocking collectives, slice_ratio(): lax.all_gather(weight_share / denom_share, 'topic', axis=0, tiled=True)  53.5 us
    ppermute x8, waiting for transfers between devices, passed_along(): return lax.ppermute(block, axis, route)  21.1 us
    psum x1, waiting for transfers between devices, shards(): word_total = lax.psum(word_local, 'dp')  15.5 us
    dot_general x12, matrix products, matmul_high(): jnp.dot(left, right, precision=lax.Precision.HIGHEST, preferred_element_t...  14.2 us
    psum x1, blocking collectives, shards(): mass = lax.psum(jnp.sum(doc_mix, axis=1), 'topic')  13.5 us
    ppermute x8, starting transfers between devices, passed_along(): return lax.ppermute(block, axis, route)  12.5 us
    div x4, other arithmetic, slice_ratio(): weight_share / denom_share  5.67 us
  transfers between devices with their start and end apart: 13, of which 9 were waited for; matrix products, arithmetic and copies ran while one was open for 8% of the time, Pallas kernels for 0%

commit v1 on v0

v1 whole, which is shorter than its diff:
```python
import functools

import jax
import jax.numpy as jnp
from jax import lax
from jax.experimental import pallas as pl
from jax.experimental.pallas import tpu as pltpu
from jax.sharding import PartitionSpec as P

VOCAB = 1048576
ALPHA = 0.1
BETA = 0.01
F32, BF16 = jnp.float32, jnp.bfloat16
MESH = pl.DeviceIdType.MESH


def partner(index, step, size):
    total, bit = 0, 1
    while bit < size:
        a, b = (index // bit) % 2, (step // bit) % 2
        total = total + bit * (a + b - 2 * a * b)
        bit *= 2
    return total


def halves(x):
    hi = x.astype(BF16)
    return hi, (x - hi.astype(F32)).astype(BF16)


def mul(a, b, dims):
    return lax.dot_general(a, b, (dims, ((), ())), preferred_element_type=F32)


def mul3(a, b, dims):
    return mul(a[0], b[0], dims) + (mul(a[0], b[1], dims) + mul(a[1], b[0], dims))


def steps(first, last, body):
    if last - first <= 4:
        for step in range(first, last):
            body(step)
    else:
        lax.fori_loop(first, last, lambda i, z: (body(i), z)[1], 0)


def kernel(
    sizes, mix, lengths, counts, tile, wc, totals, doc_out, word_out,
    mass_send, mass_in, words, w_hi, w_lo, dw, d_hi, d_lo, counts_t,
    part, part_in, ratio, wsum, pair_in, reduced, cut_in,
    mass_s, mass_r, wg_s, wg_r, wf_s, wf_r, pt_s, pt_r, rt_s, rt_r,
    c1_s, c1_r, c2_s, c2_r, c4_s, c4_r,
):
    n_dp, n_cut, n_top = sizes
    ws, width = wc.shape
    docs = mix.shape[0]
    me_p, me_c, me_t = lax.axis_index("dp"), lax.axis_index("cuts"), lax.axis_index("topic")
    rows_p, rows_t = ws // n_dp, ws // n_top

    def dp(q):
        return {"dp": partner(me_p, q, n_dp)}

    def cut(r):
        return {"cuts": partner(me_c, r, n_cut)}

    def top(q):
        return {"topic": partner(me_t, q, n_top)}

    def sl(r):
        return partner(me_c, r, n_cut)

    def p_rows(s, p):
        return pl.ds(pl.multiple_of(s * ws + p * rows_p, rows_p), rows_p)

    def t_rows(s, t):
        return pl.ds(pl.multiple_of(s * ws + t * rows_t, rows_t), rows_t)

    def s_rows(s):
        return pl.ds(pl.multiple_of(s * ws, ws), ws)

    def rc(src, dst, ss, rs, dev):
        return pltpu.make_async_remote_copy(
            src_ref=src, dst_ref=dst, send_sem=ss, recv_sem=rs,
            device_id=dev, device_id_type=MESH)

    barrier = pltpu.get_barrier_semaphore()
    for size, dev in ((n_top, top), (n_cut, cut), (n_dp, dp)):
        for q in range(1, size):
            pl.semaphore_signal(barrier, inc=1, device_id=dev(q), device_id_type=MESH)

    words[s_rows(me_c), :] = (wc[...] + BETA) / (totals[...] + VOCAB * BETA)
    col = jnp.sum(mix[...], axis=1, keepdims=True)
    mass_send[...] = jnp.broadcast_to(col, (docs, 128)).T[0:8, :]
    pl.semaphore_wait(barrier, n_top + n_cut + n_dp - 3)

    def mass_copy(q, dst_step):
        return rc(mass_send, mass_in.at[dst_step], mass_s.at[q], mass_r.at[q], top(q))

    for q in range(1, n_top):
        mass_copy(q, q).start()

    def gather(r, s):
        rows = p_rows(s, me_p)
        return rc(words.at[rows, :], words.at[rows, :], wg_s.at[r], wg_r.at[r], cut(r))

    steps(1, n_cut, lambda r: gather(r, me_c).start())

    def forward(r, q, p):
        rows = p_rows(sl(r), p)
        return rc(words.at[rows, :], words.at[rows, :], wf_s.at[r, q], wf_r.at[r, q], dp(q))

    counts_t[...] = counts[...].astype(F32).T

    w_hi[s_rows(me_c), :], w_lo[s_rows(me_c), :] = halves(words[s_rows(me_c), :])

    mass = mass_send[...]
    for q in range(1, n_top):
        mass_copy(q, q).wait_recv()
        mass = mass + mass_in[q]
    scale = lengths[...].astype(F32) / mass[0:1, :]
    scale = jnp.broadcast_to(scale, (128, docs)).T[:, 0:1]
    weight = mix[...] * scale + ALPHA
    dw[...] = weight
    d_hi[...], d_lo[...] = halves(weight)

    def part_copy(r, q, s, t):
        return rc(part.at[t_rows(s, t), :], part_in.at[r, q], pt_s.at[r, q], pt_r.at[r, q], top(q))

    def denominators(r):
        s = sl(r)
        rows = s_rows(s)
        part[rows, :] = mul3((w_hi[rows, :], w_lo[rows, :]), (d_hi[...], d_lo[...]), ((1,), (1,)))
        for q in range(1, n_top):
            part_copy(r, q, s, partner(me_t, q, n_top)).start()

    def ratio_copy(r, q, t):
        rows = t_rows(sl(r), t)
        return rc(ratio.at[rows, :], ratio.at[rows, :], rt_s.at[r, q], rt_r.at[r, q], top(q))

    def ratios(r):
        s = sl(r)
        rows = t_rows(s, me_t)
        denom = part[rows, :]
        for q in range(1, n_top):
            part_copy(r, q, s, me_t).wait_recv()
            denom = denom + part_in[r, q]
        flag = tile[0, s].astype(F32)
        ratio[rows, :] = counts_t[rows, :] * flag / denom
        for q in range(1, n_top):
            ratio_copy(r, q, me_t).start()

    def pair_copy(r, q, p):
        return rc(wsum.at[p_rows(sl(r), p), :], pair_in.at[r, q], c1_s.at[r, q], c1_r.at[r, q], dp(q))

    def word_sums(r):
        rows = s_rows(sl(r))
        for q in range(1, n_top):
            ratio_copy(r, q, partner(me_t, q, n_top)).wait_recv()
        both = halves(ratio[rows, :])
        wsum[rows, :] = mul3(both, (d_hi[...], d_lo[...]), ((1,), (0,)))
        for q in range(1, n_dp):
            pair_copy(r, q, partner(me_p, q, n_dp)).start()

    def cut_copy(r):
        return rc(reduced.at[r], cut_in.at[r], c2_s.at[r], c2_r.at[r], cut(r))

    def reduce_pair(r):
        total = wsum[p_rows(sl(r), me_p), :]
        for q in range(1, n_dp):
            pair_copy(r, q, me_p).wait_recv()
            total = total + pair_in[r, q]
        reduced[r] = total

    def send_cut(r):
        reduce_pair(r)
        cut_copy(r).start()

    denominators(0)
    ratios(0)

    def pass_on(r):
        gather(r, sl(r)).wait_recv()
        for q in range(1, n_dp):
            forward(r, q, me_p).start()

    steps(1, n_cut, pass_on)

    def take(r):
        for q in range(1, n_dp):
            forward(r, q, partner(me_p, q, n_dp)).wait_recv()
        rows = s_rows(sl(r))
        w_hi[rows, :], w_lo[rows, :] = halves(words[rows, :])
        denominators(r)

    steps(1, n_cut, take)
    word_sums(0)
    steps(1, n_cut, ratios)

    def words_then_pair(r):
        word_sums(r)

    steps(1, n_cut, words_then_pair)
    steps(1, n_cut, send_cut)
    reduce_pair(0)

    left = halves(ratio[...].T)
    chunk = min(width, 256)
    for at in range(0, width, chunk):
        cols = slice(at, at + chunk)
        sums = mul3(left, (w_hi[:, cols], w_lo[:, cols]), ((1,), (0,)))
        doc_out[:, cols] = dw[:, cols] * sums

    def add_cut(r):
        cut_copy(r).wait_recv()
        reduced[0] = reduced[0] + cut_in[r]

    steps(1, n_cut, add_cut)
    mine = pl.ds(pl.multiple_of(me_p * rows_p, rows_p), rows_p)
    word_out[mine, :] = words[p_rows(me_c, me_p), :] * reduced[0]

    def last_copy(q, p):
        rows = pl.ds(pl.multiple_of(p * rows_p, rows_p), rows_p)
        return rc(word_out.at[rows, :], word_out.at[rows, :], c4_s.at[q], c4_r.at[q], dp(q))

    for q in range(1, n_dp):
        last_copy(q, me_p).start()

    for q in range(1, n_top):
        mass_copy(q, q).wait_send()

    def settle(r):
        for q in range(1, n_top):
            part_copy(r, q, sl(r), partner(me_t, q, n_top)).wait_send()
            ratio_copy(r, q, me_t).wait_send()
        for q in range(1, n_dp):
            pair_copy(r, q, partner(me_p, q, n_dp)).wait_send()

    def settle_cut(r):
        gather(r, me_c).wait_send()
        cut_copy(r).wait_send()
        for q in range(1, n_dp):
            forward(r, q, me_p).wait_send()

    steps(0, n_cut, settle)
    steps(1, n_cut, settle_cut)
    for q in range(1, n_dp):
        last_copy(q, me_p).wait_send()
        last_copy(q, partner(me_p, q, n_dp)).wait_recv()


def shards(sizes, doc_mix, doc_lengths, counts, tile_on, word_counts, topic_totals):
    n_dp, n_cut, n_top = sizes
    docs, width = doc_mix.shape
    ws = word_counts.shape[0]
    words = counts.shape[1]
    dma = pltpu.SemaphoreType.DMA
    vm = pltpu.VMEM
    vspec = pl.BlockSpec(memory_space=pltpu.VMEM)
    return pl.pallas_call(
        functools.partial(kernel, sizes),
        out_shape=(
            jax.ShapeDtypeStruct((docs, width), F32),
            jax.ShapeDtypeStruct((ws, width), F32),
        ),
        in_specs=[vspec, vspec, vspec, pl.BlockSpec(memory_space=pltpu.SMEM), vspec, vspec],
        out_specs=(vspec, vspec),
        scratch_shapes=[
            vm((8, docs), F32),
            vm((n_top, 8, docs), F32),
            vm((words, width), F32),
            vm((words, width), BF16),
            vm((words, width), BF16),
            vm((docs, width), F32),
            vm((docs, width), BF16),
            vm((docs, width), BF16),
            vm((words, docs), F32),
            vm((words, docs), F32),
            vm((n_cut, n_top, ws // n_top, docs), F32),
            vm((words, docs), F32),
            vm((words, width), F32),
            vm((n_cut, n_dp, ws // n_dp, width), F32),
            vm((n_cut, ws // n_dp, width), F32),
            vm((n_cut, ws // n_dp, width), F32),
            dma((n_top,)), dma((n_top,)),
            dma((n_cut,)), dma((n_cut,)),
            dma((n_cut, n_dp)), dma((n_cut, n_dp)),
            dma((n_cut, n_top)), dma((n_cut, n_top)),
            dma((n_cut, n_top)), dma((n_cut, n_top)),
            dma((n_cut, n_dp)), dma((n_cut, n_dp)),
            dma((n_cut,)), dma((n_cut,)),
            dma((n_dp,)), dma((n_dp,)),
        ],
        compiler_params=pltpu.CompilerParams(
            collective_id=0, has_side_effects=True, vmem_limit_bytes=44 * 1024 * 1024),
        cost_estimate=pl.CostEstimate(
            flops=6 * docs * words * width, transcendentals=0,
            bytes_accessed=4 * (2 * docs * width + docs * words + 2 * ws * width)),
    )(doc_mix, doc_lengths[None, :], counts, tile_on, word_counts, topic_totals[None, :])


def solution(mesh):
    sizes = (mesh.shape["dp"], mesh.shape["cuts"], mesh.shape["topic"])
    return jax.shard_map(
        functools.partial(shards, sizes),
        mesh=mesh,
        in_specs=(
            P(("dp", "cuts"), "topic"),
            P(("dp", "cuts")),
            P(("dp", "cuts"), None),
            P(("dp", "cuts"), None),
            P("cuts", "topic"),
            P("topic"),
        ),
        out_specs=(P(("dp", "cuts"), "topic"), P("cuts", "topic")),
        check_vma=False,
    )
```

time: 233 us -> 45.1 us (0.19)
  waiting for transfers between devices: 106 us -> 0 us
  blocking collectives: 67 us -> 0 us
  Pallas kernels: 0 us -> 38.1 us
  between operations: 15.2 us -> 0.66 us
  matrix products: 14.2 us -> 0 us
  other arithmetic: 12.6 us -> 0 us
  starting transfers between devices: 12.5 us -> 0 us
    reduce_scatter x4 -> x0, waiting for transfers between devices: 69.3 us -> none  [slice_ratio(): lax.psum_scatter(partial_denom, 'topic', scatter_dimension=0, tiled=True)]
    all_gather x4 -> x0, blocking collectives: 53.5 us -> none  [slice_ratio(): lax.all_gather(weight_share / denom_share, 'topic', axis=0, tiled=True)]
    pallas_call x0 -> x1, Pallas kernels: none -> 38.1 us  [shards(): pl.pallas_call(functools.partial(kernel, sizes), out_shape=(jax.ShapeDtyp...]
    ppermute x8 -> x0, waiting for transfers between devices: 21.1 us -> none  [passed_along(): return lax.ppermute(block, axis, route)]
    psum x1 -> x0, waiting for transfers between devices: 15.5 us -> none  [shards(): word_total = lax.psum(word_local, 'dp')]
    dot_general x12 -> x0, matrix products: 14.2 us -> none  [matmul_high(): jnp.dot(left, right, precision=lax.Precision.HIGHEST, preferred_element_t...]
    psum x1 -> x0, blocking collectives: 13.5 us -> none  [shards(): mass = lax.psum(jnp.sum(doc_mix, axis=1), 'topic')]
    ppermute x8 -> x0, starting transfers between devices: 12.5 us -> none  [passed_along(): return lax.ppermute(block, axis, route)]
  transfers between devices with their start and end apart: 13 -> 0, of which waited for: 9 -> 0; matrix products, arithmetic and copies ran while one was open for 8% -> 0% of each run, Pallas kernels for 0% -> 0%
where the time goes in v1:
time: 45.1 us; the launch traced here: 44.9 us
  Pallas kernels  38.1 us (84%)
  local copies, waits for them, and re-layouts  6.15 us (14%)
  between operations  0.66 us (1%)
    pallas_call x1, Pallas kernels, shards(): pl.pallas_call(functools.partial(kernel, sizes), out_shape=(jax.ShapeDtyp...  38.1 us
    unnamed x14, local copies, waits for them, and re-layouts  6.15 us

profile of v1, /device:TPU:0, one launch (start us, length us, event | category | flops | bytes accessed | tf_op | source)
XLA Modules:
  0.0 44.9 jit_solution(10219446098001661058)
XLA Ops:
  0.6 0.0 copy-start.4
  0.6 0.0 copy-start.5
  0.7 0.7 %copy-done.4 = s32[256]{0:T(256)S(1)} copy-done((s32[256]{0:T(256)S(1)}, s32[256]{0:T(256)}, u32[]{:S(2)}) %copy-start.4) | copy-done | bytes 1048
  1.3 0.0 copy-done.5
  1.3 0.0 copy-start
  1.3 1.2 %copy-done = f32[256,1024]{1,0:T(8,128)S(1)} copy-done((f32[256,1024]{1,0:T(8,128)S(1)}, f32[256,1024]{1,0:T(8,128)}, u32[]{:S(2)}) %copy-start) | copy-done | bytes 1048600
  2.5 0.0 copy-start.1
  2.5 0.9 %copy-done.1 = s32[256,256]{1,0:T(8,128)S(1)} copy-done((s32[256,256]{1,0:T(8,128)S(1)}, s32[256,256]{1,0:T(8,128)}, u32[]{:S(2)}) %copy-start.1) | copy-done | bytes 262168
  3.5 0.0 copy-start.2
  3.5 0.9 %copy-done.2 = f32[64,1024]{1,0:T(8,128)S(1)} copy-done((f32[64,1024]{1,0:T(8,128)S(1)}, f32[64,1024]{1,0:T(8,128)}, u32[]{:S(2)}) %copy-start.2) | copy-done | bytes 262168
  4.4 0.0 copy-start.3
  4.4 0.7 %copy-done.3 = f32[1024]{0:T(1024)S(1)} copy-done((f32[1024]{0:T(1024)S(1)}, f32[1024]{0:T(1024)}, u32[]{:S(2)}) %copy-start.3) | copy-done | bytes 4120
  5.1 38.1 %shard_map.77 = (f32[256,1024]{1,0:T(8,128)S(1)}, f32[64,1024]{1,0:T(8,128)S(1)}) custom-call(f32[256,1024]{1,0:T(8,128)S(1)} %copy-done, s32[1,256]{1,0:T(1,128)S(1)} %bitcast.3, s32[256,256]{1,0:T(8,128)S(1)} %copy-done.1, s32[1,4]{1,0:T(1,128)S(1)} %copy-done.5, f32[64,1024]{1,0:T(8,128)S(1)} %copy-done.2, f32[1,1024]{1,0:T(1,128)S(1)} %bitcast.2), custom_call_target="tpu_custom_call" | custom-call | flops 402653184 | bytes 2883584 | tf_op jit(solution)/shard_map/pallas_call | solution.py:259
  43.2 1.0 %copy.10 = f32[256,1024]{1,0:T(8,128)} copy(f32[256,1024]{1,0:T(8,128)S(1)} %get-tuple-element.4) | data formatting | bytes 2097152
  44.2 0.7 %copy.11 = f32[64,1024]{1,0:T(8,128)} copy(f32[64,1024]{1,0:T(8,128)S(1)} %get-tuple-element.5) | data formatting | bytes 524288
Async XLA Ops:
  0.6 0.7 %copy-start.4 = (s32[256]{0:T(256)S(1)}, s32[256]{0:T(256)}, u32[]{:S(2)}) copy-start(s32[256]{0:T(256)} %param.7) | copy-start | bytes 3076
  0.6 0.7 %copy-start.5 = (s32[1,4]{1,0:T(1,128)S(1)}, s32[1,4]{1,0:T(1,128)}, u32[]{:S(2)}) copy-start(s32[1,4]{1,0:T(1,128)} %tile.1) | copy-start | bytes 52
  1.3 1.2 %copy-start = (f32[256,1024]{1,0:T(8,128)S(1)}, f32[256,1024]{1,0:T(8,128)}, u32[]{:S(2)}) copy-start(f32[256,1024]{1,0:T(8,128)} %mix.1) | copy-start | bytes 3145732
  2.5 0.9 %copy-start.1 = (s32[256,256]{1,0:T(8,128)S(1)}, s32[256,256]{1,0:T(8,128)}, u32[]{:S(2)}) copy-start(s32[256,256]{1,0:T(8,128)} %counts.1) | copy-start | bytes 786436
  3.5 0.9 %copy-start.2 = (f32[64,1024]{1,0:T(8,128)S(1)}, f32[64,1024]{1,0:T(8,128)}, u32[]{:S(2)}) copy-start(f32[64,1024]{1,0:T(8,128)} %wc.1) | copy-start | bytes 786436
  4.4 0.7 %copy-start.3 = (f32[1024]{0:T(1024)S(1)}, f32[1024]{0:T(1024)}, u32[]{:S(2)}) copy-start(f32[1024]{0:T(1024)} %param.11) | copy-start | bytes 12292

commit v2 on v1

--- a/solution.py
+++ b/solution.py
@@ -45,7 +45,8 @@
 
 
 def kernel(
-    sizes, mix, lengths, counts, tile, wc, totals, doc_out, word_out,
+    sizes, mix_h, lengths_h, counts_h, tile_h, wc_h, totals_h, doc_out, word_out,
+    mix, lengths, counts, tile, wc, totals, in_s,
     mass_send, mass_in, words, w_hi, w_lo, dw, d_hi, d_lo, counts_t,
     part, part_in, ratio, wsum, pair_in, reduced, cut_in,
     mass_s, mass_r, wg_s, wg_r, wf_s, wf_r, pt_s, pt_r, rt_s, rt_r,
@@ -88,16 +89,21 @@
         for q in range(1, size):
             pl.semaphore_signal(barrier, inc=1, device_id=dev(q), device_id_type=MESH)
 
+    loads = [
+        pltpu.make_async_copy(src, dst, in_s.at[i])
+        for i, (src, dst) in enumerate((
+            (totals_h, totals), (wc_h, wc), (mix_h, mix),
+            (lengths_h, lengths), (tile_h, tile), (counts_h, counts)))
+    ]
+    for load in loads:
+        load.start()
+    loads[0].wait()
+    loads[1].wait()
     words[s_rows(me_c), :] = (wc[...] + BETA) / (totals[...] + VOCAB * BETA)
-    col = jnp.sum(mix[...], axis=1, keepdims=True)
-    mass_send[...] = jnp.broadcast_to(col, (docs, 128)).T[0:8, :]
     pl.semaphore_wait(barrier, n_top + n_cut + n_dp - 3)
 
     def mass_copy(q, dst_step):
         return rc(mass_send, mass_in.at[dst_step], mass_s.at[q], mass_r.at[q], top(q))
-
-    for q in range(1, n_top):
-        mass_copy(q, q).start()
 
     def gather(r, s):
         rows = p_rows(s, me_p)
@@ -105,10 +111,18 @@
 
     steps(1, n_cut, lambda r: gather(r, me_c).start())
 
+    loads[2].wait()
+    col = jnp.sum(mix[...], axis=1, keepdims=True)
+    mass_send[...] = jnp.broadcast_to(col, (docs, 128)).T[0:8, :]
+    for q in range(1, n_top):
+        mass_copy(q, q).start()
+
     def forward(r, q, p):
         rows = p_rows(sl(r), p)
         return rc(words.at[rows, :], words.at[rows, :], wf_s.at[r, q], wf_r.at[r, q], dp(q))
 
+    for load in loads[3:]:
+        load.wait()
     counts_t[...] = counts[...].astype(F32).T
 
     w_hi[s_rows(me_c), :], w_lo[s_rows(me_c), :] = halves(words[s_rows(me_c), :])
@@ -144,7 +158,8 @@
         for q in range(1, n_top):
             part_copy(r, q, s, me_t).wait_recv()
             denom = denom + part_in[r, q]
-        flag = tile[0, s].astype(F32)
+        place = lax.broadcasted_iota(jnp.int32, (1, n_cut), 1)
+        flag = jnp.sum(jnp.where(place == s, tile[...], 0).astype(F32), axis=1, keepdims=True)
         ratio[rows, :] = counts_t[rows, :] * flag / denom
         for q in range(1, n_top):
             ratio_copy(r, q, me_t).start()
@@ -175,15 +190,10 @@
         reduce_pair(r)
         cut_copy(r).start()
 
-    denominators(0)
-    ratios(0)
-
     def pass_on(r):
         gather(r, sl(r)).wait_recv()
         for q in range(1, n_dp):
             forward(r, q, me_p).start()
-
-    steps(1, n_cut, pass_on)
 
     def take(r):
         for q in range(1, n_dp):
@@ -192,15 +202,33 @@
         w_hi[rows, :], w_lo[rows, :] = halves(words[rows, :])
         denominators(r)
 
-    steps(1, n_cut, take)
-    word_sums(0)
-    steps(1, n_cut, ratios)
-
-    def words_then_pair(r):
-        word_sums(r)
-
-    steps(1, n_cut, words_then_pair)
-    steps(1, n_cut, send_cut)
+    denominators(0)
+    if n_cut == 4:
+        pass_on(1)
+        pass_on(2)
+        ratios(0)
+        take(1)
+        take(2)
+        pass_on(3)
+        ratios(1)
+        take(3)
+        word_sums(0)
+        ratios(2)
+        word_sums(1)
+        ratios(3)
+        send_cut(1)
+        word_sums(2)
+        send_cut(2)
+        word_sums(3)
+        send_cut(3)
+    else:
+        ratios(0)
+        steps(1, n_cut, pass_on)
+        steps(1, n_cut, take)
+        word_sums(0)
+        steps(1, n_cut, ratios)
+        steps(1, n_cut, word_sums)
+        steps(1, n_cut, send_cut)
     reduce_pair(0)
 
     left = halves(ratio[...].T)
@@ -262,9 +290,16 @@
             jax.ShapeDtypeStruct((docs, width), F32),
             jax.ShapeDtypeStruct((ws, width), F32),
         ),
-        in_specs=[vspec, vspec, vspec, pl.BlockSpec(memory_space=pltpu.SMEM), vspec, vspec],
+        in_specs=[pl.BlockSpec(memory_space=pltpu.HBM)] * 6,
         out_specs=(vspec, vspec),
         scratch_shapes=[
+            vm((docs, width), F32),
+            vm((1, docs), jnp.int32),
+            vm((docs, words), jnp.int32),
+            vm((1, n_cut), jnp.int32),
+            vm((ws, width), F32),
+            vm((1, width), F32),
+            dma((6,)),
             vm((8, docs), F32),
             vm((n_top, 8, docs), F32),
             vm((words, width), F32),
@@ -291,7 +326,7 @@
             dma((n_dp,)), dma((n_dp,)),
         ],
         compiler_params=pltpu.CompilerParams(
-            collective_id=0, has_side_effects=True, vmem_limit_bytes=44 * 1024 * 1024),
+            collective_id=0, has_side_effects=True, vmem_limit_bytes=62 * 1024 * 1024),
         cost_estimate=pl.CostEstimate(
             flops=6 * docs * words * width, transcendentals=0,
             bytes_accessed=4 * (2 * docs * width + docs * words + 2 * ws * width)),

time: 45.1 us -> 42.1 us (0.933)
  local copies, waits for them, and re-layouts: 6.15 us -> 3.06 us
    unnamed x14 -> x4, local copies, waits for them, and re-layouts: 6.15 us -> 3.06 us
where the time goes in v2:
time: 42.1 us; the launch traced here: 41.9 us
  Pallas kernels  38.2 us (91%)
  local copies, waits for them, and re-layouts  3.06 us (7%)
  between operations  0.65 us (2%)
    pallas_call x1, Pallas kernels, shards(): pl.pallas_call(functools.partial(kernel, sizes), out_shape=(jax.ShapeDtyp...  38.2 us
    unnamed x4, local copies, waits for them, and re-layouts  3.06 us

profile of v2, /device:TPU:0, one launch (start us, length us, event | category | flops | bytes accessed | tf_op | source)
XLA Modules:
  0.0 41.9 jit_solution(10971113034117608862)
XLA Ops:
  0.6 38.2 %shard_map.77 = (f32[256,1024]{1,0:T(8,128)}, f32[64,1024]{1,0:T(8,128)}) custom-call(f32[256,1024]{1,0:T(8,128)} %mix_h.1, s32[1,256]{1,0:T(1,128)} %bitcast.3, s32[256,256]{1,0:T(8,128)} %counts_h.1, s32[1,4]{1,0:T(1,128)} %tile_h.1, f32[64,1024]{1,0:T(8,128)} %wc_h.1, f32[1,1024]{1,0:T(1,128)} %bitcast.2), custom_call_target="tpu_custom_call" | custom-call | flops 402653184 | bytes 2883584 | tf_op jit(solution)/shard_map/pallas_call | solution.py:287
  38.8 0.0 copy-start
  38.9 2.3 %copy.10 = f32[256,1024]{1,0:T(8,128)} copy(f32[256,1024]{1,0:T(8,128)} %get-tuple-element.4) | data formatting | bytes 2097152
  41.2 0.0 copy-done
  41.2 0.7 %copy.11 = f32[64,1024]{1,0:T(8,128)} copy(f32[64,1024]{1,0:T(8,128)S(1)} %copy-done) | data formatting | bytes 524288
Async XLA Ops:
  38.8 2.4 %copy-start = (f32[64,1024]{1,0:T(8,128)S(1)}, f32[64,1024]{1,0:T(8,128)}, u32[]{:S(2)}) copy-start(f32[64,1024]{1,0:T(8,128)} %get-tuple-element.5) | copy-start | bytes 786436
